TPU v7x, 32 devices: a whole 2x2x4 slice. The times are simulated.
32 devices in a mesh: ka: 8 (over z, y), ga: 4 (over x, core).
Axes of the slice: x: 2, y: 2, z: 4, core: 2. Of those that a mesh axis runs over, the one named last changes fastest.
Arguments:
- cond_pairs: bfloat16 [4, 48, 2, 16, 1024], P(None, 'ka', None, None, 'ga'), may hold values from -1 to 1
- val_pairs: bfloat16 [4, 48, 2, 16, 1024], P(None, 'ka', None, None, 'ga'), may hold values from -1 to 1
- screened: bfloat16 [4, 2, 1024, 1024], P(None, None, 'ka', 'ga'), may hold values from -1 to 4, as said below
- k_plus: int32 [4, 48], replicated, may hold values from 0 to 47, as said below
Outputs:
- kernel_forward: float32 [4, 48, 2, 256], P(None, 'ka', None, 'ga')
- kernel_back: float32 [4, 48, 2, 256], P(None, 'ka', None, 'ga')
Inputs may be any that keep to these rules, and one draw needn't show every extreme that they name: screened[q, 0] is symmetric and screened[q, 1] antisymmetric in the last two dimensions, so W(q) is Hermitian. For each q there is one translation (dx, dy) of the periodic 4 x 12 grid, with k = x * 12 + y, such that k_plus[q, k] = ((x + dx) mod 4) * 12 + (y + dy) mod 12.
All inputs are finite; a program needn't handle non-finite values.
Results may differ from a plain program's by a relative error of at most 0.0029.
Values may be sent and summed in bfloat16 or wider, within the bound.
A program may use at most 64 MiB of HBM per device.

v0:
```python
import jax
import jax.numpy as jnp
from jax import lax
from jax.sharding import PartitionSpec as P

NG = 1024
Q = 4
CPAIR = 16
VPAIR = 16


def passed_along(block, axis, distance):
    devices = range(lax.axis_size(axis))
    route = [((i - distance) % len(devices), i) for i in devices]
    return lax.ppermute(block, axis, route)


def swapped(shard, axis, bit):
    return lax.ppermute(shard, axis, [(i, i ^ 1 << bit) for i in range(lax.axis_size(axis))])


def screen_fold(left_real, left_imag, piece):
    real_next = jnp.dot(left_real, piece[0], preferred_element_type=jnp.float32) + jnp.dot(
        left_imag, piece[1], preferred_element_type=jnp.float32
    )
    imag_next = jnp.dot(left_real, piece[1], preferred_element_type=jnp.float32) - jnp.dot(
        left_imag, piece[0], preferred_element_type=jnp.float32
    )
    return (real_next, imag_next)


def pair_contract(left, right):
    return jnp.einsum("kag,kbg->kab", left, right, preferred_element_type=jnp.float32)


def local(cond_pairs, val_pairs, screened, k_plus):
    local_k = cond_pairs.shape[1]
    columns = screened.shape[3]
    grid_y = 2 * local_k
    forward = []
    for q_index in range(Q):
        cond_full = lax.all_gather(cond_pairs[q_index], "ga", axis=3, tiled=True)
        left_real = cond_full[:, 0].reshape(local_k * CPAIR, NG)
        left_imag = cond_full[:, 1].reshape(local_k * CPAIR, NG)
        real_x, imag_x = screen_fold(
            left_real, left_imag, lax.all_gather(screened[q_index], "ka", axis=1, tiled=True)
        )
        real_b = real_x.astype(jnp.bfloat16).reshape(local_k, CPAIR, columns)
        imag_b = imag_x.astype(jnp.bfloat16).reshape(local_k, CPAIR, columns)
        val_real = val_pairs[q_index][:, 0]
        val_imag = val_pairs[q_index][:, 1]
        kernel_real = pair_contract(real_b, val_real) - pair_contract(imag_b, val_imag)
        kernel_imag = pair_contract(real_b, val_imag) + pair_contract(imag_b, val_real)
        forward.append(jnp.stack([kernel_real, kernel_imag], 1).reshape(local_k, 2, CPAIR * VPAIR))
    partial_value = jnp.stack(forward, 0)
    total = lax.psum(partial_value, "ga")
    width = total.shape[3] // lax.axis_size("ga")
    kernel_share = lax.dynamic_slice_in_dim(total, lax.axis_index("ga") * width, width, 3)
    count = lax.axis_size("ka")
    corner = k_plus[:, 0]
    row_step = corner // grid_y
    col_step = corner % grid_y
    hop_length = 2 * row_step % count
    moved = kernel_share
    nbits = count.bit_length() - 1
    for bit_number in range(1, nbits):
        arrived = passed_along(moved, "ka", 1 << bit_number)
        taken = hop_length // (1 << bit_number) % 2 == 1
        moved = jnp.where(taken[:, None, None, None], arrived, moved)
    partner = swapped(moved, "ka", 0)
    half_index = lax.axis_index("ka") % 2
    whole_row = jnp.where(
        half_index == 0, jnp.concatenate([moved, partner], 1), jnp.concatenate([partner, moved], 1)
    )
    doubled = jnp.concatenate([whole_row, whole_row], 1)
    backs = []
    for q_index in range(Q):
        begin = (half_index * local_k - col_step[q_index] + grid_y) % grid_y
        backs.append(lax.dynamic_slice_in_dim(doubled[q_index], begin, local_k, 0))
    kernel_back = jnp.stack(backs, 0)
    return (kernel_share, kernel_back)


def solution(mesh):
    in_specs = (
        P(None, "ka", None, None, "ga"),
        P(None, "ka", None, None, "ga"),
        P(None, None, "ka", "ga"),
        P(),
    )
    out_specs = (P(None, "ka", None, "ga"), P(None, "ka", None, "ga"))
    return jax.shard_map(local, mesh=mesh, in_specs=in_specs, out_specs=out_specs, check_vma=False)
```

profile of v0, /device:TPU:0, one launch (start us, length us, event | category | flops | bytes accessed | tf_op | source)
XLA Modules:
  0.0 223.2 jit_solution(4785162403844171694)
XLA Ops:
  7.2 1.9 fusion.31
  11.7 7.9 %all-gather = bf16[1,6,2,16,1024]{4,3,2,1,0:T(8,128)(2,1)S(1)} all-gather(bf16[1,6,2,16,256]{4,3,2,1,0:T(8,128)(2,1)S(1)} %get-tuple-element.18), channel_id=2, replica_groups=mesh['ka'=8,'ga'=4] {'ga'}, dimensions={4}, use_global_device_ids=true | all-gather | bytes 491520 | tf_op jit(solution)/shard_map/all_gather | solution.py:42
  19.6 1.0 copy-done.16
  20.7 6.6 %all-gather.2 = bf16[1,6,2,16,1024]{4,3,2,1,0:T(8,128)(2,1)S(1)} all-gather(bf16[1,6,2,16,256]{4,3,2,1,0:T(8,128)(2,1)S(1)} %get-tuple-element.19), channel_id=4, replica_groups=mesh['ka'=8,'ga'=4] {'ga'}, dimensions={4}, use_global_device_ids=true | all-gather | bytes 491520 | tf_op jit(solution)/shard_map/all_gather | solution.py:42
  27.3 6.6 %all-gather.4 = bf16[1,6,2,16,1024]{4,3,2,1,0:T(8,128)(2,1)S(1)} all-gather(bf16[1,6,2,16,256]{4,3,2,1,0:T(8,128)(2,1)S(1)} %get-tuple-element.21), channel_id=6, replica_groups=mesh['ka'=8,'ga'=4] {'ga'}, dimensions={4}, use_global_device_ids=true | all-gather | bytes 491520 | tf_op jit(solution)/shard_map/all_gather | solution.py:42
  33.9 6.6 %all-gather.6 = bf16[1,6,2,16,1024]{4,3,2,1,0:T(8,128)(2,1)S(1)} all-gather(bf16[1,6,2,16,256]{4,3,2,1,0:T(8,128)(2,1)S(1)} %get-tuple-element.20), channel_id=8, replica_groups=mesh['ka'=8,'ga'=4] {'ga'}, dimensions={4}, use_global_device_ids=true | all-gather | bytes 491520 | tf_op jit(solution)/shard_map/all_gather | solution.py:42
  40.6 12.5 %all-gather.13.cloned.1.call-done = bf16[1,2,1024,256]{3,2,1,0:T(8,128)(2,1)} async-done(((bf16[1,2,128,256]{3,2,1,0:T(8,128)(2,1)}), bf16[1,2,1024,256]{3,2,1,0:T(8,128)(2,1)}) %all-gather.13.cloned.1.call-update) | async-done | bytes 1048592 | tf_op jit(solution)/shard_map/all_gather | solution.py:46
  53.1 1.3 fusion.8
  54.4 1.3 fusion
  55.6 0.7 fusion.16
  56.4 37.9 %all-gather.15.cloned.1.call-done = bf16[1,2,1024,256]{3,2,1,0:T(8,128)(2,1)} async-done(((bf16[1,2,128,256]{3,2,1,0:T(8,128)(2,1)}), bf16[1,2,1024,256]{3,2,1,0:T(8,128)(2,1)}) %all-gather.15.cloned.1.call-update) | async-done | bytes 1048592 | tf_op jit(solution)/shard_map/all_gather | solution.py:46
  94.3 1.3 fusion.10
  95.5 0.7 fusion.17
  96.3 1.3 fusion.2
  97.6 0.7 fusion.18
  98.3 0.7 fusion.19
  99.0 36.5 %all-gather.17.cloned.1.call-done = bf16[1,2,1024,256]{3,2,1,0:T(8,128)(2,1)} async-done(((bf16[1,2,128,256]{3,2,1,0:T(8,128)(2,1)}), bf16[1,2,1024,256]{3,2,1,0:T(8,128)(2,1)}) %all-gather.17.cloned.1.call-update) | async-done | bytes 1048592 | tf_op jit(solution)/shard_map/all_gather | solution.py:46
  135.5 1.3 fusion.12
  136.8 1.3 fusion.4
  138.1 0.8 fusion.20
  138.8 0.7 fusion.21
  139.6 37.0 %all-gather.19.cloned.1.call-done = bf16[1,2,1024,256]{3,2,1,0:T(8,128)(2,1)} async-done(((bf16[1,2,128,256]{3,2,1,0:T(8,128)(2,1)}), bf16[1,2,1024,256]{3,2,1,0:T(8,128)(2,1)}) %all-gather.19.cloned.1.call-update) | async-done | bytes 1048592 | tf_op jit(solution)/shard_map/all_gather | solution.py:46
  176.5 1.3 fusion.14
  177.8 1.3 fusion.6
  179.1 0.7 fusion.22
  179.8 0.7 fusion.23
  181.1 0.7 copy-done.13
  183.4 0.7 copy-done.11
  185.8 0.7 copy-done.9
  190.0 10.7 %psum.7 = f32[4,6,2,256]{3,1,2,0:T(8,128)S(1)} all-reduce(f32[4,6,2,256]{3,1,2,0:T(8,128)S(1)} %maximum_maximum_fusion), channel_id=1, replica_groups=mesh['ka'=8,'ga'=4] {'ga'}, use_global_device_ids=true, to_apply=%region_0.0 | all-reduce | flops 12288 | bytes 98304 | tf_op jit(solution)/shard_map/psum | solution.py:56
  201.5 5.0 %collective-permute-done = f32[4,6,2,64]{3,1,2,0:T(8,128)S(1)} collective-permute-done((f32[4,6,2,64]{3,1,2,0:T(8,128)S(1)}, f32[4,6,2,64]{3,1,2,0:T(8,128)S(1)}, u32[]{:S(2)}, u32[]{:S(2)}) %collective-permute-start) | collective-permute-done | bytes 12320 | tf_op jit(solution)/shard_map/ppermute | solution.py:15
  206.6 4.8 %collective-permute-done.1 = f32[4,6,2,64]{3,1,2,0:T(8,128)S(1)} collective-permute-done((f32[4,6,2,64]{3,1,2,0:T(8,128)S(1)}, f32[4,6,2,64]{3,1,2,0:T(8,128)S(1)}, u32[]{:S(2)}, u32[]{:S(2)}) %collective-permute-start.1) | collective-permute-done | bytes 12320 | tf_op jit(solution)/shard_map/ppermute | solution.py:15
  (111 shorter events, 13.3 us)
Async XLA Ops:
  7.2 45.9 %all-gather.13.cloned.1.call-start = ((), (), s32[]{:S(2)}) async-start(), calls=%async_computation | async-start | bytes 1179648 | tf_op jit(solution)/shard_map/all_gather | solution.py:46
  9.1 2.5 %copy-start.15 = (bf16[4,6,2,16,256]{4,3,2,1,0:T(8,128)(2,1)S(1)}, bf16[4,6,2,16,256]{4,3,2,1,0:T(8,128)(2,1)}, u32[]{:S(2)}) copy-start(bf16[4,6,2,16,256]{4,3,2,1,0:T(8,128)(2,1)} %param.4) | copy-start | bytes 1179652
  9.2 85.1 %all-gather.15.cloned.1.call-start = ((), (), s32[]{:S(2)}) async-start(), calls=%async_computation.1 | async-start | bytes 1179648 | tf_op jit(solution)/shard_map/all_gather | solution.py:46
  9.9 125.6 %all-gather.17.cloned.1.call-start = ((), (), s32[]{:S(2)}) async-start(), calls=%async_computation.2 | async-start | bytes 1179648 | tf_op jit(solution)/shard_map/all_gather | solution.py:46
  10.6 165.9 %all-gather.19.cloned.1.call-start = ((), (), s32[]{:S(2)}) async-start(), calls=%async_computation.3 | async-start | bytes 1179648 | tf_op jit(solution)/shard_map/all_gather | solution.py:46
  19.6 1.0 copy-start.16
  20.6 32.5 %copy-start.4 = (bf16[6,1,16,1024]{3,2,1,0:T(8,128)(2,1)}, bf16[6,1,16,1024]{3,2,1,0:T(8,128)(2,1)S(1)}, u32[]{:S(2)}) copy-start(bf16[6,1,16,1024]{3,2,1,0:T(8,128)(2,1)S(1)} %get-tuple-element.17) | copy-start | bytes 589828
  20.6 74.9 %copy-start.12 = (bf16[1,6,2,16,256]{4,3,1,2,0:T(8,128)(2,1)}, bf16[1,6,2,16,256]{4,3,1,2,0:T(8,128)(2,1)S(1)}, u32[]{:S(2)}) copy-start(bf16[1,6,2,16,256]{4,3,1,2,0:T(8,128)(2,1)S(1)} %copy.35) | copy-start | bytes 294916
  27.3 71.0 %copy-start.10 = (bf16[1,6,2,16,256]{4,3,1,2,0:T(8,128)(2,1)}, bf16[1,6,2,16,256]{4,3,1,2,0:T(8,128)(2,1)S(1)}, u32[]{:S(2)}) copy-start(bf16[1,6,2,16,256]{4,3,1,2,0:T(8,128)(2,1)S(1)} %copy.34) | copy-start | bytes 294916
  33.9 104.9 %copy-start.8 = (bf16[1,6,2,16,256]{4,3,1,2,0:T(8,128)(2,1)}, bf16[1,6,2,16,256]{4,3,1,2,0:T(8,128)(2,1)S(1)}, u32[]{:S(2)}) copy-start(bf16[1,6,2,16,256]{4,3,1,2,0:T(8,128)(2,1)S(1)} %copy.33) | copy-start | bytes 294916
  40.5 139.3 %copy-start.6 = (bf16[1,6,2,16,256]{4,3,1,2,0:T(8,128)(2,1)}, bf16[1,6,2,16,256]{4,3,1,2,0:T(8,128)(2,1)S(1)}, u32[]{:S(2)}) copy-start(bf16[1,6,2,16,256]{4,3,1,2,0:T(8,128)(2,1)S(1)} %copy.32) | copy-start | bytes 294916
  138.8 41.8 %copy-start.3 = (bf16[1,2,1024,256]{3,2,1,0:T(8,128)(2,1)S(1)}, bf16[1,2,1024,256]{3,2,1,0:T(8,128)(2,1)}, u32[]{:S(2)}) copy-start(bf16[1,2,1024,256]{3,2,1,0:T(8,128)(2,1)} %all-gather.13.cloned.1.call-done) | copy-start | bytes 3145732
  179.1 1.5 copy-start.5
  180.6 2.4 %copy-start.2 = (bf16[1,2,1024,256]{3,2,1,0:T(8,128)(2,1)S(1)}, bf16[1,2,1024,256]{3,2,1,0:T(8,128)(2,1)}, u32[]{:S(2)}) copy-start(bf16[1,2,1024,256]{3,2,1,0:T(8,128)(2,1)} %all-gather.15.cloned.1.call-done) | copy-start | bytes 3145732
  180.8 1.0 copy-start.13
  180.8 1.0 copy-start.23
  181.8 0.9 copy-start.14
  181.9 0.8 copy-start.24
  183.0 2.4 %copy-start.1 = (bf16[1,2,1024,256]{3,2,1,0:T(8,128)(2,1)S(1)}, bf16[1,2,1024,256]{3,2,1,0:T(8,128)(2,1)}, u32[]{:S(2)}) copy-start(bf16[1,2,1024,256]{3,2,1,0:T(8,128)(2,1)} %all-gather.17.cloned.1.call-done) | copy-start | bytes 3145732
  183.2 1.0 copy-start.11
  183.2 1.0 copy-start.22
  184.3 0.8 copy-start.21
  185.3 2.4 %copy-start = (bf16[1,2,1024,256]{3,2,1,0:T(8,128)(2,1)S(1)}, bf16[1,2,1024,256]{3,2,1,0:T(8,128)(2,1)}, u32[]{:S(2)}) copy-start(bf16[1,2,1024,256]{3,2,1,0:T(8,128)(2,1)} %all-gather.19.cloned.1.call-done) | copy-start | bytes 3145732
  185.6 1.0 copy-start.9
  185.6 1.0 copy-start.20
  186.7 0.8 copy-start.19
  187.9 0.9 copy-start.7
  187.9 0.9 copy-start.18
  189.0 0.8 copy-start.17
  200.8 5.7 %collective-permute-start = (f32[4,6,2,64]{3,1,2,0:T(8,128)S(1)}, f32[4,6,2,64]{3,1,2,0:T(8,128)S(1)}, u32[]{:S(2)}, u32[]{:S(2)}) collective-permute-start(f32[4,6,2,64]{3,1,2,0:T(8,128)S(1)} %constant_dynamic-slice_fusion), channel_id=1, source_target_pairs={{24,0},{28,4},{0,8},{4,12},{8,16},{12,20},{16,24},{20,28},{25,1},{... | collective-permute-start | bytes 36872 | tf_op jit(solution)/shard_map/ppermute | solution.py:15
  206.6 4.9 %collective-permute-start.1 = (f32[4,6,2,64]{3,1,2,0:T(8,128)S(1)}, f32[4,6,2,64]{3,1,2,0:T(8,128)S(1)}, u32[]{:S(2)}, u32[]{:S(2)}) collective-permute-start(f32[4,6,2,64]{3,1,2,0:T(8,128)S(1)} %broadcast_select_fusion), channel_id=1, source_target_pairs={{16,0},{20,4},{24,8},{28,12},{0,16},{4,20},{8,24},{12,28},{17,1},{... | collective-permute-start | bytes 36872 | tf_op jit(solution)/shard_map/ppermute | solution.py:15
  211.5 4.4 %collective-permute-start.2 = (f32[4,6,2,64]{3,1,2,0:T(8,128)S(1)}, f32[4,6,2,64]{3,1,2,0:T(8,128)S(1)}, u32[]{:S(2)}, u32[]{:S(2)}) collective-permute-start(f32[4,6,2,64]{3,1,2,0:T(8,128)S(1)} %broadcast_select_fusion.1), channel_id=1, source_target_pairs={{0,4},{4,0},{8,12},{12,8},{16,20},{20,16},{24,28},{28,24},{1,5},{5... | collective-permute-start | bytes 36872 | tf_op jit(solution)/shard_map/ppermute | solution.py:19
  (1 other events, 0.7 us)
Sparse Core Ops, SparseCore 0:
  10.2 42.8 all-gather.12
  55.3 38.9 all-gather.14
  96.5 39.0 all-gather.16
  137.6 38.9 all-gather.18
where the time goes:
time: 224 us; the launch traced here: 223 us
  waiting for transfers between devices  136 us (61%)
  blocking collectives  38.3 us (17%)
  matrix products  18.8 us (8%)
  between operations  16.8 us (8%)
  local copies, waits for them, and re-layouts  11.6 us (5%)
    all_gather x4, waiting for transfers between devices, local(): lax.all_gather(screened[q_index], 'ka', axis=1, tiled=True)  124 us
    all_gather x4, blocking collectives, local(): cond_full = lax.all_gather(cond_pairs[q_index], 'ga', axis=3, tiled=True)  27.6 us
    psum x1, blocking collectives, local(): total = lax.psum(partial_value, 'ga')  10.7 us
    ppermute x2, waiting for transfers between devices, passed_along(): return lax.ppermute(block, axis, route)  9.78 us
    unnamed x58, local copies, waits for them, and re-layouts  8.16 us
    dot_general x16, matrix products, pair_contract(): jnp.einsum('kag,kbg->kab', left, right, preferred_element_type=jnp.float32)  6.93 us
    dot_general x4, matrix products, screen_fold(): jnp.dot(left_imag, piece[1], preferred_element_type=jnp.float32)  5.06 us
    dot_general x4, matrix products, screen_fold(): jnp.dot(left_real, piece[0], preferred_element_type=jnp.float32)  5.04 us
  transfers between devices with their start and end apart: 7, of which 6 were waited for; matrix products, arithmetic and copies ran while one was open for 6% of the time, Pallas kernels for 0%

commit v1 on v0

--- a/solution.py
+++ b/solution.py
@@ -1,12 +1,350 @@
+import functools
+
 import jax
 import jax.numpy as jnp
 from jax import lax
+from jax.experimental import pallas as pl
+from jax.experimental.pallas import tpu as pltpu
 from jax.sharding import PartitionSpec as P
+
+MESH = pl.DeviceIdType.MESH
+HIGHEST = lax.Precision.HIGHEST
+F32 = jnp.float32
+BF16 = jnp.bfloat16
+
+
+def nearest_source(pair, dest):
+    i, j = pair
+    if abs(i - dest) == abs(j - dest):
+        return i if i in (0,) or j == dest + 1 and i == dest - 1 and dest < 2 else j
+    return i if abs(i - dest) < abs(j - dest) else j
+
+
+def block_plan(rows):
+    squares, others = [], []
+    for dest in range(rows):
+        squares.append(sorted(((i, i) for i in range(rows) if i != dest), key=lambda b: abs(b[0] - dest)))
+        blocks = []
+        for i in range(rows):
+            for j in range(i + 1, rows):
+                if dest not in (i, j):
+                    src = nearest_source((i, j), dest)
+                    blocks.append((src, i + j - src))
+        others.append(sorted(blocks, key=lambda b: abs(b[0] - dest)))
+    return squares, others
+
+
+def pick(index, values):
+    out = jnp.int32(values[0])
+    for n in range(1, len(values)):
+        out = jnp.where(index == n, jnp.int32(values[n]), out)
+    return out
+
+
+def nt(a, b):
+    return lax.dot_general(a, b, (((1,), (1,)), ((), ())), preferred_element_type=F32)
+
+
+def kernel(
+    rows, c_ref, v_ref, w_ref, kp_ref, f_ref, b_ref,
+    wall, cbuf, vbuf, lhs, mix, vl, xacc, kown, ksib, kstage, kall,
+    w1s, w1r, cs, cr, vs, vr, cfs, vfs, zs, zr, ks, kr, os, orr,
+):
+    kpd, npair = cbuf.shape[2], cbuf.shape[4]
+    half = wall.shape[3]
+    mrows = 2 * kpd * npair
+    ka, g = lax.axis_index("ka"), lax.axis_index("ga")
+    z, y = ka // 2, ka % 2
+    x, h = g // 2, g % 2
+    mine = 2 * x + y
+
+    def dev(zz, yy, xx, hh):
+        return (2 * zz + yy, 2 * xx + hh)
+
+    def remote(src, dst, ssem, rsem, target):
+        return pltpu.make_async_remote_copy(
+            src_ref=src, dst_ref=dst, send_sem=ssem, recv_sem=rsem, device_id=target, device_id_type=MESH
+        )
+
+    barrier = pltpu.get_barrier_semaphore()
+    count = 0
+    for dz in range(rows):
+        for dy in range(2):
+            for dx in range(2):
+                for dh in range(2):
+                    if (dz and dh) or not (dz or dy or dx or dh):
+                        continue
+                    pl.semaphore_signal(
+                        barrier, inc=1,
+                        device_id=dev((z + dz) % rows, (y + dy) % 2, (x + dx) % 2, (h + dh) % 2),
+                        device_id_type=MESH,
+                    )
+                    count += 1
+    pl.semaphore_wait(barrier, count)
+
+    steps = [(1, 1), (1, 0), (0, 1), (0, 0)]
+
+    def w_copy(n):
+        dy, dx = steps[n]
+        qy, qx = (y + dy) % 2, (x + dx) % 2
+        return remote(w_ref.at[2 * qx + qy], wall.at[z, g], w1s.at[n], w1r.at[g], dev(z, qy, qx, y))
+
+    for n in range(3):
+        w_copy(n).start()
+
+    @pl.when(h == y)
+    def _():
+        pltpu.make_async_copy(w_ref.at[mine], wall.at[z, g], w1r.at[g]).start()
+
+    @pl.when(h != y)
+    def _():
+        w_copy(3).start()
+
+    def pair_copy(ref, buf, ssem, rsem, n):
+        dy, dx = steps[n]
+        qy, qx = (y + dy) % 2, (x + dx) % 2
+        return remote(ref.at[2 * qx + qy], buf.at[y, g], ssem.at[n], rsem.at[y, g], dev(z, qy, qx, h))
+
+    xacc[...] = jnp.zeros_like(xacc)
+
+    for j in range(rows):
+        pltpu.make_async_copy(wall.at[z, j], wall.at[z, j], w1r.at[j]).wait()
+
+    squares, others = block_plan(rows)
+    sends = [[] for _ in range(rows)]
+    for dest in range(rows):
+        for i, j in squares[dest] + others[dest]:
+            sends[i].append((dest, j))
+
+    def z_copies(src):
+        order = sorted(sends[src], key=lambda s: (abs(s[0] - src), s[1] == src))
+        for n, (dest, j) in enumerate(order):
+            yield remote(wall.at[src, j], wall.at[src, j], zs.at[n], zr.at[src, j], dev(dest, y, x, h))
+
+    for src in range(rows):
+        @pl.when(z == src)
+        def _():
+            for copy in z_copies(src):
+                copy.start()
+
+    for ref, buf, ssem, rsem in ((c_ref, cbuf, cs, cr), (v_ref, vbuf, vs, vr)):
+        for n in range(3):
+            pair_copy(ref, buf, ssem, rsem, n).start()
+        pltpu.make_async_copy(ref.at[mine], buf.at[y, g], rsem.at[y, g]).start()
+
+    def hand_on(buf, ssem, rsem, yy, xx):
+        slot = buf.at[yy, 2 * xx + h]
+        return remote(slot, slot, ssem.at[yy, xx], rsem.at[yy, 2 * xx + h], dev(z, y, x, 1 - h))
+
+    def arrived(buf, rsem, yy, j):
+        pltpu.make_async_copy(buf.at[yy, j], buf.at[yy, j], rsem.at[yy, j]).wait()
+
+    for buf, rsem, fsem in ((cbuf, cr, cfs), (vbuf, vr, vfs)):
+        for dy in range(2):
+            for dx in range(2):
+                yy, xx = (y + dy) % 2, (x + dx) % 2
+                arrived(buf, rsem, yy, 2 * xx + h)
+                hand_on(buf, fsem, rsem, yy, xx).start()
+
+    def stacked(buf, rsem, out):
+        for yy in range(2):
+            for xx in range(2):
+                arrived(buf, rsem, yy, 2 * xx + 1 - h)
+        for j in range(rows):
+            for yy in range(2):
+                for part in range(2):
+                    block = buf[yy, j, :, part].reshape(kpd * npair, 2 * half)
+                    out[j, pl.ds((2 * part + yy) * kpd * npair, kpd * npair), :] = block
+
+    lanes = pl.ds(pl.multiple_of(h * half, half), half)
+    stacked(cbuf, cr, lhs)
+    for j in range(rows):
+        both = lhs[j, :, lanes]
+        real, imag = both[:mrows], both[mrows:]
+        mix[j, :mrows, :half] = real
+        mix[j, :mrows, half:] = imag
+        mix[j, mrows:, :half] = -imag
+        mix[j, mrows:, half:] = real
+
+    def plain(i, j):
+        w = wall[i, j].reshape(2 * half, 2 * half)
+        xacc[j] += jnp.dot(mix[i], w, preferred_element_type=F32)
+
+    def adjoint(i, j):
+        w = wall[i, j].reshape(2 * half, 2 * half)
+        p = nt(lhs[j], w)
+        xacc[i, :mrows, lanes] += p[:mrows, :half] - p[mrows:, half:]
+        xacc[i, mrows:, lanes] -= p[:mrows, half:] + p[mrows:, :half]
+
+    plain(z, z)
+    for n in range(1, rows):
+        j = (z + n) % rows
+        plain(z, j)
+        adjoint(z, j)
+
+    stacked(vbuf, vr, vl)
+
+    nsq, noth = len(squares[0]), len(others[0])
+    for n in range(max(nsq, noth)):
+        if n < nsq:
+            i = pick(z, [s[n][0] for s in squares])
+            pltpu.make_async_copy(wall.at[i, i], wall.at[i, i], zr.at[i, i]).wait()
+            plain(i, i)
+        if n < noth:
+            i = pick(z, [s[n][0] for s in others])
+            j = pick(z, [s[n][1] for s in others])
+            pltpu.make_async_copy(wall.at[i, j], wall.at[i, j], zr.at[i, j]).wait()
+            plain(i, j)
+            adjoint(i, j)
+
+    with_real = jnp.zeros((2 * mrows, mrows), F32)
+    with_imag = jnp.zeros((2 * mrows, mrows), F32)
+    for j in range(rows):
+        total = xacc[j]
+        high = total.astype(BF16)
+        low = (total - high.astype(F32)).astype(BF16)
+        vreal, vimag = vl[j, :mrows], vl[j, mrows:]
+        with_real += nt(high, vreal) + nt(low, vreal)
+        with_imag += nt(high, vimag) + nt(low, vimag)
+    kreal = with_real[:mrows] - with_imag[mrows:]
+    kimag = with_imag[:mrows] + with_real[mrows:]
+
+    width = npair * npair
+    row = lax.broadcasted_iota(jnp.int32, (mrows, mrows), 0)
+    col = lax.broadcasted_iota(jnp.int32, (mrows, mrows), 1)
+    same_k = lax.div(row, npair) == lax.div(col, npair)
+    vrow = lax.broadcasted_iota(jnp.int32, (mrows, width), 0)
+    lane = lax.broadcasted_iota(jnp.int32, (mrows, width), 1)
+    spread = jnp.where(lax.rem(vrow, npair) == lax.rem(lane, npair), 1.0, 0.0).astype(F32)
+    same_a = lax.rem(vrow, npair) == lax.div(lane, npair)
+    kgrid = mrows // npair
+    for part, value in enumerate((kreal, kimag)):
+        wide = jnp.dot(jnp.where(same_k, value, 0.0), spread, precision=HIGHEST, preferred_element_type=F32)
+        wide = jnp.where(same_a, wide, 0.0).reshape(kgrid, npair, width)
+        kown[pl.ds(part * kgrid, kgrid), :] = wide.sum(1)
+
+    pair_sum = remote(kown, ksib, ks, kr, dev(z, y, x, 1 - h))
+    pair_sum.start()
+    pair_sum.wait()
+    total = kown[...] + ksib[...]
+    share = kstage.shape[2]
+    for n in range(kstage.shape[0]):
+        kstage[n] = total[:, n * share:(n + 1) * share]
+
+    def out_copies():
+        n = 0
+        for dz in range(rows):
+            for dy in range(2):
+                for dx in range(2):
+                    if dz or dy or dx:
+                        zz, yy, xx = (z + dz) % rows, (y + dy) % 2, (x + dx) % 2
+                        yield remote(
+                            kstage.at[2 * xx + h], kall.at[mine, z], os.at[n], orr.at[mine, z], dev(zz, yy, xx, h)
+                        )
+                        n += 1
+
+    for copy in out_copies():
+        copy.start()
+    kall[mine, z] = kstage[g]
+    for dz in range(rows):
+        for dy in range(2):
+            for dx in range(2):
+                if dz or dy or dx:
+                    zz = (z + dz) % rows
+                    qq = 2 * ((x + dx) % 2) + (y + dy) % 2
+                    pltpu.make_async_copy(kall.at[qq, zz], kall.at[qq, zz], orr.at[qq, zz]).wait()
+
+    outs = f_ref.shape[1]
+    o = lax.broadcasted_iota(jnp.int32, (outs, rows * 2 * kgrid), 0)
+    r = lax.broadcasted_iota(jnp.int32, (outs, rows * 2 * kgrid), 1)
+    k_here = y * kpd + lax.div(o, 2)
+    part_at = lax.rem(o, 2) * kgrid
+    ahead = jnp.where(r == z * 2 * kgrid + part_at + k_here, 1.0, 0.0).astype(F32)
+    for q in range(kall.shape[0]):
+        table = kall[q].reshape(rows * 2 * kgrid, share)
+        corner = kp_ref[q, 0]
+        row_step = lax.div(corner, kgrid)
+        col_step = lax.rem(corner, kgrid)
+        src_row = lax.rem(z - row_step + rows, rows)
+        src_col = lax.rem(k_here - col_step + kgrid, kgrid)
+        behind = jnp.where(r == src_row * 2 * kgrid + part_at + src_col, 1.0, 0.0).astype(F32)
+        f_ref[q] = jnp.dot(ahead, table, precision=HIGHEST, preferred_element_type=F32)
+        b_ref[q] = jnp.dot(behind, table, precision=HIGHEST, preferred_element_type=F32)
+
+    for n in range(3):
+        w_copy(n).wait_send()
+        pair_copy(c_ref, cbuf, cs, cr, n).wait_send()
+        pair_copy(v_ref, vbuf, vs, vr, n).wait_send()
+
+    @pl.when(h != y)
+    def _():
+        w_copy(3).wait_send()
+
+    for src in range(rows):
+        @pl.when(z == src)
+        def _():
+            for copy in z_copies(src):
+                copy.wait_send()
+
+    for buf, rsem, fsem in ((cbuf, cr, cfs), (vbuf, vr, vfs)):
+        for dy in range(2):
+            for dx in range(2):
+                hand_on(buf, fsem, rsem, (y + dy) % 2, (x + dx) % 2).wait_send()
+    for copy in out_copies():
+        copy.wait_send()
+
+
+def exchanged(cond_pairs, val_pairs, screened, k_plus):
+    nq, kpd, _, npair, cols = cond_pairs.shape
+    half = screened.shape[2]
+    rows = lax.axis_size("ka") // 2
+    ga = lax.axis_size("ga")
+    mrows = 2 * kpd * npair
+    width = npair * npair
+    share = width // ga
+    dma = pltpu.SemaphoreType.DMA
+    out = jax.ShapeDtypeStruct((nq, 2 * kpd, share), F32)
+    squares, others = block_plan(rows)
+    most = max(
+        sum(i == src for d in range(rows) for i, _ in squares[d] + others[d]) for src in range(rows)
+    )
+    forward, back = pl.pallas_call(
+        functools.partial(kernel, rows),
+        out_shape=(out, out),
+        in_specs=[pl.BlockSpec(memory_space=pl.ANY)] * 3 + [pl.BlockSpec(memory_space=pltpu.SMEM)],
+        out_specs=[pl.BlockSpec(memory_space=pltpu.VMEM)] * 2,
+        scratch_shapes=[
+            pltpu.VMEM((rows, rows, 2, half, cols), BF16),
+            pltpu.VMEM((2, ga, kpd, 2, npair, cols), BF16),
+            pltpu.VMEM((2, ga, kpd, 2, npair, cols), BF16),
+            pltpu.VMEM((ga, 2 * mrows, cols), BF16),
+            pltpu.VMEM((ga, 2 * mrows, cols), BF16),
+            pltpu.VMEM((ga, 2 * mrows, cols), BF16),
+            pltpu.VMEM((ga, 2 * mrows, cols), F32),
+            pltpu.VMEM((4 * kpd, width), F32),
+            pltpu.VMEM((4 * kpd, width), F32),
+            pltpu.VMEM((ga, 4 * kpd, share), F32),
+            pltpu.VMEM((nq, rows, 4 * kpd, share), F32),
+            dma((4,)), dma((ga,)),
+            dma((3,)), dma((2, ga)),
+            dma((3,)), dma((2, ga)),
+            dma((2, 2)), dma((2, 2)),
+            dma((most,)), dma((rows, rows)),
+            dma, dma,
+            dma((4 * rows - 1,)), dma((nq, rows)),
+        ],
+        compiler_params=pltpu.CompilerParams(
+            collective_id=0, has_side_effects=True, vmem_limit_bytes=40 * 1024 * 1024
+        ),
+    )(cond_pairs, val_pairs, screened, k_plus)
+    shape = (nq, kpd, 2, share)
+    return forward.reshape(shape), back.reshape(shape)
+
 
 NG = 1024
 Q = 4
-CPAIR = 16
-VPAIR = 16
+npair = 16
+npair = 16
 
 
 def passed_along(block, axis, distance):
@@ -34,24 +372,25 @@
 
 
 def local(cond_pairs, val_pairs, screened, k_plus):
-    local_k = cond_pairs.shape[1]
+    nq, local_k, _, npair, own = cond_pairs.shape
+    ng = own * lax.axis_size("ga")
     columns = screened.shape[3]
     grid_y = 2 * local_k
     forward = []
-    for q_index in range(Q):
+    for q_index in range(nq):
         cond_full = lax.all_gather(cond_pairs[q_index], "ga", axis=3, tiled=True)
-        left_real = cond_full[:, 0].reshape(local_k * CPAIR, NG)
-        left_imag = cond_full[:, 1].reshape(local_k * CPAIR, NG)
+        left_real = cond_full[:, 0].reshape(local_k * npair, ng)
+        left_imag = cond_full[:, 1].reshape(local_k * npair, ng)
         real_x, imag_x = screen_fold(
             left_real, left_imag, lax.all_gather(screened[q_index], "ka", axis=1, tiled=True)
         )
-        real_b = real_x.astype(jnp.bfloat16).reshape(local_k, CPAIR, columns)
-        imag_b = imag_x.astype(jnp.bfloat16).reshape(local_k, CPAIR, columns)
+        real_b = real_x.astype(jnp.bfloat16).reshape(local_k, npair, columns)
+        imag_b = imag_x.astype(jnp.bfloat16).reshape(local_k, npair, columns)
         val_real = val_pairs[q_index][:, 0]
         val_imag = val_pairs[q_index][:, 1]
         kernel_real = pair_contract(real_b, val_real) - pair_contract(imag_b, val_imag)
         kernel_imag = pair_contract(real_b, val_imag) + pair_contract(imag_b, val_real)
-        forward.append(jnp.stack([kernel_real, kernel_imag], 1).reshape(local_k, 2, CPAIR * VPAIR))
+        forward.append(jnp.stack([kernel_real, kernel_imag], 1).reshape(local_k, 2, npair * npair))
     partial_value = jnp.stack(forward, 0)
     total = lax.psum(partial_value, "ga")
     width = total.shape[3] // lax.axis_size("ga")
@@ -74,7 +413,7 @@
     )
     doubled = jnp.concatenate([whole_row, whole_row], 1)
     backs = []
-    for q_index in range(Q):
+    for q_index in range(nq):
         begin = (half_index * local_k - col_step[q_index] + grid_y) % grid_y
         backs.append(lax.dynamic_slice_in_dim(doubled[q_index], begin, local_k, 0))
     kernel_back = jnp.stack(backs, 0)
@@ -89,4 +428,6 @@
         P(),
     )
     out_specs = (P(None, "ka", None, "ga"), P(None, "ka", None, "ga"))
-    return jax.shard_map(local, mesh=mesh, in_specs=in_specs, out_specs=out_specs, check_vma=False)
+    square = mesh.shape["ga"] == 4 and mesh.shape["ka"] == 2 * mesh.shape["ga"]
+    body = exchanged if square else local
+    return jax.shard_map(body, mesh=mesh, in_specs=in_specs, out_specs=out_specs, check_vma=False)

time: 224 us -> 50.4 us (0.23)
  waiting for transfers between devices: 136 us -> 0 us
  Pallas kernels: 0 us -> 44.4 us
  blocking collectives: 38.3 us -> 0 us
  matrix products: 18.8 us -> 0 us
  between operations: 16.8 us -> 0.66 us
  local copies, waits for them, and re-layouts: 11.6 us -> 4.97 us
    all_gather x4 -> x0, waiting for transfers between devices: 124 us -> none  [local(): lax.all_gather(screened[q_index], 'ka', axis=1, tiled=True)]
    pallas_call x0 -> x1, Pallas kernels: none -> 44.4 us  [exchanged(): pl.pallas_call(functools.partial(kernel, rows), out_shape=(out, out), in_...]
    all_gather x4 -> x0, blocking collectives: 27.6 us -> none  [local(): cond_full = lax.all_gather(cond_pairs[q_index], 'ga', axis=3, tiled=True)]
    dot_general x32 -> x0, matrix products: 18.8 us -> none  [the longest x16 6.93 us: pair_contract(): jnp.einsum('kag,kbg->kab', left, right, preferred_element_type=jnp.float32)]
    psum x1 -> x0, blocking collectives: 10.7 us -> none  [local(): total = lax.psum(partial_value, 'ga')]
    ppermute x3 -> x0, waiting for transfers between devices: 9.79 us -> none  [the longest x2 9.78 us: passed_along(): return lax.ppermute(block, axis, route)]
    unnamed x58 -> x10, local copies, waits for them, and re-layouts: 8.16 us -> 4.95 us
    slice x9 -> x0, local copies, waits for them, and re-layouts: 2.71 us -> none  [the longest x1 1.91 us: local(): screened[q_index]]
  transfers between devices with their start and end apart: 7 -> 0, of which waited for: 6 -> 0; matrix products, arithmetic and copies ran while one was open for 6% -> 0% of each run, Pallas kernels for 0% -> 0%
where the time goes in v1:
time: 50.4 us; the launch traced here: 50.1 us
  Pallas kernels  44.4 us (88%)
  local copies, waits for them, and re-layouts  4.97 us (10%)
  between operations  0.66 us (1%)
    pallas_call x1, Pallas kernels, exchanged(): pl.pallas_call(functools.partial(kernel, rows), out_shape=(out, out), in_...  44.4 us
    unnamed x10, local copies, waits for them, and re-layouts  4.95 us

profile of v1, /device:TPU:0, one launch (start us, length us, event | category | flops | bytes accessed | tf_op | source)
XLA Modules:
  0.0 50.1 jit_solution(14091266575597285569)
XLA Ops:
  0.6 0.0 copy-start
  0.6 1.0 %copy-done = bf16[4,2,128,256]{3,2,1,0:T(8,128)(2,1)S(1)} copy-done((bf16[4,2,128,256]{3,2,1,0:T(8,128)(2,1)S(1)}, bf16[4,2,128,256]{3,2,1,0:T(8,128)(2,1)}, u32[]{:S(2)}) %copy-start) | copy-done | bytes 524312
  1.7 0.0 copy-start.1
  1.7 1.0 %copy-done.1 = bf16[4,6,2,16,256]{4,3,2,1,0:T(8,128)(2,1)S(1)} copy-done((bf16[4,6,2,16,256]{4,3,2,1,0:T(8,128)(2,1)S(1)}, bf16[4,6,2,16,256]{4,3,2,1,0:T(8,128)(2,1)}, u32[]{:S(2)}) %copy-start.1) | copy-done | bytes 393240
  2.7 0.0 copy-start.2
  2.7 1.0 %copy-done.2 = bf16[4,6,2,16,256]{4,3,2,1,0:T(8,128)(2,1)S(1)} copy-done((bf16[4,6,2,16,256]{4,3,2,1,0:T(8,128)(2,1)S(1)}, bf16[4,6,2,16,256]{4,3,2,1,0:T(8,128)(2,1)}, u32[]{:S(2)}) %copy-start.2) | copy-done | bytes 393240
  3.7 0.0 copy-start.3
  3.7 0.7 %copy-done.3 = s32[4,48]{1,0:T(4,128)S(1)} copy-done((s32[4,48]{1,0:T(4,128)S(1)}, s32[4,48]{1,0:T(4,128)}, u32[]{:S(2)}) %copy-start.3) | copy-done | bytes 792
  4.3 44.4 %shard_map.59 = (f32[4,12,64]{2,1,0:T(8,128)S(1)}, f32[4,12,64]{2,1,0:T(8,128)S(1)}) custom-call(bf16[4,6,2,16,256]{4,3,2,1,0:T(8,128)(2,1)S(1)} %copy-done.1, bf16[4,6,2,16,256]{4,3,2,1,0:T(8,128)(2,1)S(1)} %copy-done.2, bf16[4,2,128,256]{3,2,1,0:T(8,128)(2,1)S(1)} %copy-done, s32[4,48]{1,0:T(4,128)S(1)} %copy-done.3), custom_call_target="tpu_custom_call" | custom-call | tf_op jit(solution)/shard_map/pallas_call | solution.py:311
  48.8 0.6 %copy.8 = f32[4,6,2,64]{3,2,1,0:T(2,128)} copy(f32[4,6,2,64]{3,0,2,1:T(4,128)S(1)} %bitcast.2) | data formatting | bytes 24576
  49.5 0.6 %copy.9 = f32[4,6,2,64]{3,2,1,0:T(2,128)} copy(f32[4,6,2,64]{3,0,2,1:T(4,128)S(1)} %bitcast.3) | data formatting | bytes 24576
  (2 shorter events, 0.0 us)
Async XLA Ops:
  0.6 1.0 %copy-start = (bf16[4,2,128,256]{3,2,1,0:T(8,128)(2,1)S(1)}, bf16[4,2,128,256]{3,2,1,0:T(8,128)(2,1)}, u32[]{:S(2)}) copy-start(bf16[4,2,128,256]{3,2,1,0:T(8,128)(2,1)} %w_ref.1) | copy-start | bytes 1572868
  1.7 1.0 %copy-start.1 = (bf16[4,6,2,16,256]{4,3,2,1,0:T(8,128)(2,1)S(1)}, bf16[4,6,2,16,256]{4,3,2,1,0:T(8,128)(2,1)}, u32[]{:S(2)}) copy-start(bf16[4,6,2,16,256]{4,3,2,1,0:T(8,128)(2,1)} %c_ref.1) | copy-start | bytes 1179652
  2.7 1.0 %copy-start.2 = (bf16[4,6,2,16,256]{4,3,2,1,0:T(8,128)(2,1)S(1)}, bf16[4,6,2,16,256]{4,3,2,1,0:T(8,128)(2,1)}, u32[]{:S(2)}) copy-start(bf16[4,6,2,16,256]{4,3,2,1,0:T(8,128)(2,1)} %v_ref.1) | copy-start | bytes 1179652
  3.7 0.7 %copy-start.3 = (s32[4,48]{1,0:T(4,128)S(1)}, s32[4,48]{1,0:T(4,128)}, u32[]{:S(2)}) copy-start(s32[4,48]{1,0:T(4,128)} %kp_ref.1) | copy-start | bytes 2308

commit v2 on v1

--- a/solution.py
+++ b/solution.py
@@ -16,7 +16,7 @@
 def nearest_source(pair, dest):
     i, j = pair
     if abs(i - dest) == abs(j - dest):
-        return i if i in (0,) or j == dest + 1 and i == dest - 1 and dest < 2 else j
+        return i if i == 0 else j
     return i if abs(i - dest) < abs(j - dest) else j
 
 
@@ -47,7 +47,7 @@
 
 def kernel(
     rows, c_ref, v_ref, w_ref, kp_ref, f_ref, b_ref,
-    wall, cbuf, vbuf, lhs, mix, vl, xacc, kown, ksib, kstage, kall,
+    wall, packed, cbuf, vbuf, lhs, mix, vl, xacc, kown, ksib, kstage, kall,
     w1s, w1r, cs, cr, vs, vr, cfs, vfs, zs, zr, ks, kr, os, orr,
 ):
     kpd, npair = cbuf.shape[2], cbuf.shape[4]
@@ -107,25 +107,34 @@
 
     xacc[...] = jnp.zeros_like(xacc)
 
-    for j in range(rows):
-        pltpu.make_async_copy(wall.at[z, j], wall.at[z, j], w1r.at[j]).wait()
-
     squares, others = block_plan(rows)
     sends = [[] for _ in range(rows)]
     for dest in range(rows):
         for i, j in squares[dest] + others[dest]:
             sends[i].append((dest, j))
 
-    def z_copies(src):
-        order = sorted(sends[src], key=lambda s: (abs(s[0] - src), s[1] == src))
+    at_row = h * half + lax.broadcasted_iota(jnp.int32, (half, 2 * half), 0)
+    at_col = lax.broadcasted_iota(jnp.int32, (half, 2 * half), 1)
+
+    def z_copies(src, which=None):
+        order = sorted(sends[src], key=lambda s: (s[1], -abs(s[0] - src)))
         for n, (dest, j) in enumerate(order):
-            yield remote(wall.at[src, j], wall.at[src, j], zs.at[n], zr.at[src, j], dev(dest, y, x, h))
-
-    for src in range(rows):
-        @pl.when(z == src)
-        def _():
-            for copy in z_copies(src):
-                copy.start()
+            if which is None or j == which:
+                ref = packed.at[src] if j == src else wall.at[src, j]
+                yield remote(ref, ref, zs.at[n], zr.at[src, j], dev(dest, y, x, h))
+
+    for j in range(rows):
+        pltpu.make_async_copy(wall.at[z, j], wall.at[z, j], w1r.at[j]).wait()
+        for src in range(rows):
+            @pl.when(z == src)
+            def _():
+                if j == src:
+                    upper = at_col >= at_row
+                    packed[src] = jnp.where(
+                        upper, wall[src, src, 0].astype(F32), wall[src, src, 1].astype(F32)
+                    ).astype(BF16)
+                for copy in z_copies(src, j):
+                    copy.start()
 
     for ref, buf, ssem, rsem in ((c_ref, cbuf, cs, cr), (v_ref, vbuf, vs, vr)):
         for n in range(3):
@@ -166,21 +175,22 @@
         mix[j, mrows:, :half] = -imag
         mix[j, mrows:, half:] = real
 
-    def plain(i, j):
-        w = wall[i, j].reshape(2 * half, 2 * half)
+    def plain(i, j, w):
         xacc[j] += jnp.dot(mix[i], w, preferred_element_type=F32)
 
-    def adjoint(i, j):
-        w = wall[i, j].reshape(2 * half, 2 * half)
+    def adjoint(i, j, w):
         p = nt(lhs[j], w)
         xacc[i, :mrows, lanes] += p[:mrows, :half] - p[mrows:, half:]
         xacc[i, mrows:, lanes] -= p[:mrows, half:] + p[mrows:, :half]
 
-    plain(z, z)
+    def block(i, j):
+        return wall[i, j].reshape(2 * half, 2 * half)
+
+    plain(z, z, block(z, z))
     for n in range(1, rows):
         j = (z + n) % rows
-        plain(z, j)
-        adjoint(z, j)
+        plain(z, j, block(z, j))
+        adjoint(z, j, block(z, j))
 
     stacked(vbuf, vr, vl)
 
@@ -188,14 +198,19 @@
     for n in range(max(nsq, noth)):
         if n < nsq:
             i = pick(z, [s[n][0] for s in squares])
-            pltpu.make_async_copy(wall.at[i, i], wall.at[i, i], zr.at[i, i]).wait()
-            plain(i, i)
+            pltpu.make_async_copy(packed.at[i], packed.at[i], zr.at[i, i]).wait()
+            both = packed[i].astype(F32)
+            real = jnp.where(at_col >= at_row, both, 0.0).astype(BF16)
+            above = jnp.where(at_col > at_row, both, 0.0).astype(BF16)
+            imag = jnp.where(at_col < at_row, both, 0.0).astype(BF16)
+            plain(i, i, jnp.concatenate([real, imag], 0))
+            adjoint(i, i, jnp.concatenate([above, imag], 0))
         if n < noth:
             i = pick(z, [s[n][0] for s in others])
             j = pick(z, [s[n][1] for s in others])
             pltpu.make_async_copy(wall.at[i, j], wall.at[i, j], zr.at[i, j]).wait()
-            plain(i, j)
-            adjoint(i, j)
+            plain(i, j, block(i, j))
+            adjoint(i, j, block(i, j))
 
     with_real = jnp.zeros((2 * mrows, mrows), F32)
     with_imag = jnp.zeros((2 * mrows, mrows), F32)
@@ -254,7 +269,7 @@
                     qq = 2 * ((x + dx) % 2) + (y + dy) % 2
                     pltpu.make_async_copy(kall.at[qq, zz], kall.at[qq, zz], orr.at[qq, zz]).wait()
 
-    outs = f_ref.shape[1]
+    outs = 2 * kpd
     o = lax.broadcasted_iota(jnp.int32, (outs, rows * 2 * kgrid), 0)
     r = lax.broadcasted_iota(jnp.int32, (outs, rows * 2 * kgrid), 1)
     k_here = y * kpd + lax.div(o, 2)
@@ -268,8 +283,10 @@
         src_row = lax.rem(z - row_step + rows, rows)
         src_col = lax.rem(k_here - col_step + kgrid, kgrid)
         behind = jnp.where(r == src_row * 2 * kgrid + part_at + src_col, 1.0, 0.0).astype(F32)
-        f_ref[q] = jnp.dot(ahead, table, precision=HIGHEST, preferred_element_type=F32)
-        b_ref[q] = jnp.dot(behind, table, precision=HIGHEST, preferred_element_type=F32)
+        for ref, choice in ((f_ref, ahead), (b_ref, behind)):
+            chosen = jnp.dot(choice, table, precision=HIGHEST, preferred_element_type=F32)
+            for t in range(kpd):
+                ref[q, t] = chosen[2 * t:2 * t + 2]
 
     for n in range(3):
         w_copy(n).wait_send()
@@ -303,18 +320,19 @@
     width = npair * npair
     share = width // ga
     dma = pltpu.SemaphoreType.DMA
-    out = jax.ShapeDtypeStruct((nq, 2 * kpd, share), F32)
+    out = jax.ShapeDtypeStruct((nq, kpd, 2, share), F32)
     squares, others = block_plan(rows)
     most = max(
         sum(i == src for d in range(rows) for i, _ in squares[d] + others[d]) for src in range(rows)
     )
-    forward, back = pl.pallas_call(
+    return pl.pallas_call(
         functools.partial(kernel, rows),
         out_shape=(out, out),
-        in_specs=[pl.BlockSpec(memory_space=pl.ANY)] * 3 + [pl.BlockSpec(memory_space=pltpu.SMEM)],
+        in_specs=[pl.BlockSpec(memory_space=pltpu.HBM)] * 3 + [pl.BlockSpec(memory_space=pltpu.SMEM)],
         out_specs=[pl.BlockSpec(memory_space=pltpu.VMEM)] * 2,
         scratch_shapes=[
             pltpu.VMEM((rows, rows, 2, half, cols), BF16),
+            pltpu.VMEM((rows, half, cols), BF16),
             pltpu.VMEM((2, ga, kpd, 2, npair, cols), BF16),
             pltpu.VMEM((2, ga, kpd, 2, npair, cols), BF16),
             pltpu.VMEM((ga, 2 * mrows, cols), BF16),
@@ -334,11 +352,9 @@
             dma((4 * rows - 1,)), dma((nq, rows)),
         ],
         compiler_params=pltpu.CompilerParams(
-            collective_id=0, has_side_effects=True, vmem_limit_bytes=40 * 1024 * 1024
+            collective_id=0, has_side_effects=True, vmem_limit_bytes=64 * 1024 * 1024
         ),
     )(cond_pairs, val_pairs, screened, k_plus)
-    shape = (nq, kpd, 2, share)
-    return forward.reshape(shape), back.reshape(shape)
 
 
 NG = 1024

time: 50.4 us -> 43.5 us (0.86)
  Pallas kernels: 44.4 us -> 40.6 us
  local copies, waits for them, and re-layouts: 4.97 us -> 1.97 us
    pallas_call x1, Pallas kernels: 44.4 us -> 40.6 us  [exchanged(): pl.pallas_call(functools.partial(kernel, rows), out_shape=(out, out), in_...]
    unnamed x10 -> x4, local copies, waits for them, and re-layouts: 4.95 us -> 1.97 us
where the time goes in v2:
time: 43.5 us; the launch traced here: 43.2 us
  Pallas kernels  40.6 us (93%)
  local copies, waits for them, and re-layouts  1.97 us (5%)
  between operations  0.65 us (1%)
    pallas_call x1, Pallas kernels, exchanged(): pl.pallas_call(functools.partial(kernel, rows), out_shape=(out, out), in_...  40.6 us
    unnamed x4, local copies, waits for them, and re-layouts  1.97 us

profile of v2, /device:TPU:0, one launch (start us, length us, event | category | flops | bytes accessed | tf_op | source)
XLA Modules:
  0.0 43.2 jit_solution(15049689294136807910)
XLA Ops:
  0.6 40.6 %shard_map.59 = (f32[4,6,2,64]{3,2,1,0:T(2,128)}, f32[4,6,2,64]{3,2,1,0:T(2,128)}) custom-call(bf16[4,6,2,16,256]{4,3,2,1,0:T(8,128)(2,1)} %c_ref.1, bf16[4,6,2,16,256]{4,3,2,1,0:T(8,128)(2,1)} %v_ref.1, bf16[4,2,128,256]{3,2,1,0:T(8,128)(2,1)} %w_ref.1, s32[4,48]{1,0:T(4,128)} %kp_ref.1), custom_call_target="tpu_custom_call" | custom-call | tf_op jit(solution)/shard_map/pallas_call | solution.py:328
  41.3 0.0 copy-start
  41.3 1.4 %copy.8 = f32[4,6,2,64]{3,2,1,0:T(2,128)} copy(f32[4,6,2,64]{3,2,1,0:T(2,128)} %get-tuple-element.4) | data formatting | bytes 24576
  42.6 0.0 copy-done
  42.6 0.6 %copy.9 = f32[4,6,2,64]{3,2,1,0:T(2,128)} copy(f32[4,6,2,64]{3,2,1,0:T(2,128)S(1)} %copy-done) | data formatting | bytes 24576
Async XLA Ops:
  41.3 1.4 %copy-start = (f32[4,6,2,64]{3,2,1,0:T(2,128)S(1)}, f32[4,6,2,64]{3,2,1,0:T(2,128)}, u32[]{:S(2)}) copy-start(f32[4,6,2,64]{3,2,1,0:T(2,128)} %get-tuple-element.5) | copy-start | bytes 36868

commit v3 on v2

--- a/solution.py
+++ b/solution.py
@@ -46,7 +46,7 @@
 
 
 def kernel(
-    rows, c_ref, v_ref, w_ref, kp_ref, f_ref, b_ref,
+    rows, c_ref, v_ref, w_ref, all_ref,
     wall, packed, cbuf, vbuf, lhs, mix, vl, xacc, kown, ksib, kstage, kall,
     w1s, w1r, cs, cr, vs, vr, cfs, vfs, zs, zr, ks, kr, os, orr,
 ):
@@ -84,21 +84,24 @@
 
     steps = [(1, 1), (1, 0), (0, 1), (0, 0)]
 
-    def w_copy(n):
+    def w_copy(n, part):
         dy, dx = steps[n]
         qy, qx = (y + dy) % 2, (x + dx) % 2
-        return remote(w_ref.at[2 * qx + qy], wall.at[z, g], w1s.at[n], w1r.at[g], dev(z, qy, qx, y))
-
-    for n in range(3):
-        w_copy(n).start()
-
-    @pl.when(h == y)
-    def _():
-        pltpu.make_async_copy(w_ref.at[mine], wall.at[z, g], w1r.at[g]).start()
-
-    @pl.when(h != y)
-    def _():
-        w_copy(3).start()
+        return remote(
+            w_ref.at[2 * qx + qy, part], wall.at[z, g, part], w1s.at[n, part], w1r.at[g, part], dev(z, qy, qx, y)
+        )
+
+    for part in range(2):
+        for n in range(3):
+            w_copy(n, part).start()
+
+        @pl.when(h == y)
+        def _():
+            pltpu.make_async_copy(w_ref.at[mine, part], wall.at[z, g, part], w1r.at[g, part]).start()
+
+        @pl.when(h != y)
+        def _():
+            w_copy(3, part).start()
 
     def pair_copy(ref, buf, ssem, rsem, n):
         dy, dx = steps[n]
@@ -106,6 +109,11 @@
         return remote(ref.at[2 * qx + qy], buf.at[y, g], ssem.at[n], rsem.at[y, g], dev(z, qy, qx, h))
 
     xacc[...] = jnp.zeros_like(xacc)
+
+    for ref, buf, ssem, rsem in ((c_ref, cbuf, cs, cr), (v_ref, vbuf, vs, vr)):
+        for n in range(3):
+            pair_copy(ref, buf, ssem, rsem, n).start()
+        pltpu.make_async_copy(ref.at[mine], buf.at[y, g], rsem.at[y, g]).start()
 
     squares, others = block_plan(rows)
     sends = [[] for _ in range(rows)]
@@ -119,27 +127,25 @@
     def z_copies(src, which=None):
         order = sorted(sends[src], key=lambda s: (s[1], -abs(s[0] - src)))
         for n, (dest, j) in enumerate(order):
-            if which is None or j == which:
-                ref = packed.at[src] if j == src else wall.at[src, j]
-                yield remote(ref, ref, zs.at[n], zr.at[src, j], dev(dest, y, x, h))
-
-    for j in range(rows):
-        pltpu.make_async_copy(wall.at[z, j], wall.at[z, j], w1r.at[j]).wait()
-        for src in range(rows):
-            @pl.when(z == src)
-            def _():
-                if j == src:
-                    upper = at_col >= at_row
-                    packed[src] = jnp.where(
-                        upper, wall[src, src, 0].astype(F32), wall[src, src, 1].astype(F32)
-                    ).astype(BF16)
-                for copy in z_copies(src, j):
-                    copy.start()
-
-    for ref, buf, ssem, rsem in ((c_ref, cbuf, cs, cr), (v_ref, vbuf, vs, vr)):
-        for n in range(3):
-            pair_copy(ref, buf, ssem, rsem, n).start()
-        pltpu.make_async_copy(ref.at[mine], buf.at[y, g], rsem.at[y, g]).start()
+            for part in range(2):
+                if which is not None and (j, part) != which or j == src and part == 0:
+                    continue
+                ref = packed.at[src] if j == src else wall.at[src, j, part]
+                yield remote(ref, ref, zs.at[n, part], zr.at[src, j, part], dev(dest, y, x, h))
+
+    for part in range(2):
+        for j in range(rows):
+            pltpu.make_async_copy(wall.at[z, j, part], wall.at[z, j, part], w1r.at[j, part]).wait()
+            for src in range(rows):
+                @pl.when(z == src)
+                def _():
+                    if j == src and part == 1:
+                        upper = at_col >= at_row
+                        packed[src] = jnp.where(
+                            upper, wall[src, src, 0].astype(F32), wall[src, src, 1].astype(F32)
+                        ).astype(BF16)
+                    for copy in z_copies(src, (j, part)):
+                        copy.start()
 
     def hand_on(buf, ssem, rsem, yy, xx):
         slot = buf.at[yy, 2 * xx + h]
@@ -196,21 +202,22 @@
 
     nsq, noth = len(squares[0]), len(others[0])
     for n in range(max(nsq, noth)):
+        if n < noth:
+            i = pick(z, [s[n][0] for s in others])
+            j = pick(z, [s[n][1] for s in others])
+            for part in range(2):
+                pltpu.make_async_copy(wall.at[i, j, part], wall.at[i, j, part], zr.at[i, j, part]).wait()
+            plain(i, j, block(i, j))
+            adjoint(i, j, block(i, j))
         if n < nsq:
             i = pick(z, [s[n][0] for s in squares])
-            pltpu.make_async_copy(packed.at[i], packed.at[i], zr.at[i, i]).wait()
+            pltpu.make_async_copy(packed.at[i], packed.at[i], zr.at[i, i, 1]).wait()
             both = packed[i].astype(F32)
             real = jnp.where(at_col >= at_row, both, 0.0).astype(BF16)
             above = jnp.where(at_col > at_row, both, 0.0).astype(BF16)
             imag = jnp.where(at_col < at_row, both, 0.0).astype(BF16)
             plain(i, i, jnp.concatenate([real, imag], 0))
             adjoint(i, i, jnp.concatenate([above, imag], 0))
-        if n < noth:
-            i = pick(z, [s[n][0] for s in others])
-            j = pick(z, [s[n][1] for s in others])
-            pltpu.make_async_copy(wall.at[i, j], wall.at[i, j], zr.at[i, j]).wait()
-            plain(i, j, block(i, j))
-            adjoint(i, j, block(i, j))
 
     with_real = jnp.zeros((2 * mrows, mrows), F32)
     with_imag = jnp.zeros((2 * mrows, mrows), F32)
@@ -269,6 +276,38 @@
                     qq = 2 * ((x + dx) % 2) + (y + dy) % 2
                     pltpu.make_async_copy(kall.at[qq, zz], kall.at[qq, zz], orr.at[qq, zz]).wait()
 
+    all_ref[...] = kall[...]
+
+    for n in range(3):
+        for part in range(2):
+            w_copy(n, part).wait_send()
+        pair_copy(c_ref, cbuf, cs, cr, n).wait_send()
+        pair_copy(v_ref, vbuf, vs, vr, n).wait_send()
+
+    @pl.when(h != y)
+    def _():
+        for part in range(2):
+            w_copy(3, part).wait_send()
+
+    for src in range(rows):
+        @pl.when(z == src)
+        def _():
+            for copy in z_copies(src):
+                copy.wait_send()
+
+    for buf, rsem, fsem in ((cbuf, cr, cfs), (vbuf, vr, vfs)):
+        for dy in range(2):
+            for dx in range(2):
+                hand_on(buf, fsem, rsem, (y + dy) % 2, (x + dx) % 2).wait_send()
+    for copy in out_copies():
+        copy.wait_send()
+
+
+def choose(rows, kp_ref, kall, f_ref, b_ref):
+    kpd, share = f_ref.shape[1], f_ref.shape[3]
+    kgrid = 2 * kpd
+    ka = lax.axis_index("ka")
+    z, y = ka // 2, ka % 2
     outs = 2 * kpd
     o = lax.broadcasted_iota(jnp.int32, (outs, rows * 2 * kgrid), 0)
     r = lax.broadcasted_iota(jnp.int32, (outs, rows * 2 * kgrid), 1)
@@ -288,28 +327,6 @@
             for t in range(kpd):
                 ref[q, t] = chosen[2 * t:2 * t + 2]
 
-    for n in range(3):
-        w_copy(n).wait_send()
-        pair_copy(c_ref, cbuf, cs, cr, n).wait_send()
-        pair_copy(v_ref, vbuf, vs, vr, n).wait_send()
-
-    @pl.when(h != y)
-    def _():
-        w_copy(3).wait_send()
-
-    for src in range(rows):
-        @pl.when(z == src)
-        def _():
-            for copy in z_copies(src):
-                copy.wait_send()
-
-    for buf, rsem, fsem in ((cbuf, cr, cfs), (vbuf, vr, vfs)):
-        for dy in range(2):
-            for dx in range(2):
-                hand_on(buf, fsem, rsem, (y + dy) % 2, (x + dx) % 2).wait_send()
-    for copy in out_copies():
-        copy.wait_send()
-
 
 def exchanged(cond_pairs, val_pairs, screened, k_plus):
     nq, kpd, _, npair, cols = cond_pairs.shape
@@ -325,11 +342,11 @@
     most = max(
         sum(i == src for d in range(rows) for i, _ in squares[d] + others[d]) for src in range(rows)
     )
-    return pl.pallas_call(
+    blocks = pl.pallas_call(
         functools.partial(kernel, rows),
-        out_shape=(out, out),
-        in_specs=[pl.BlockSpec(memory_space=pltpu.HBM)] * 3 + [pl.BlockSpec(memory_space=pltpu.SMEM)],
-        out_specs=[pl.BlockSpec(memory_space=pltpu.VMEM)] * 2,
+        out_shape=jax.ShapeDtypeStruct((nq, rows, 4 * kpd, share), F32),
+        in_specs=[pl.BlockSpec(memory_space=pltpu.HBM)] * 3,
+        out_specs=pl.BlockSpec(memory_space=pltpu.VMEM),
         scratch_shapes=[
             pltpu.VMEM((rows, rows, 2, half, cols), BF16),
             pltpu.VMEM((rows, half, cols), BF16),
@@ -343,18 +360,24 @@
             pltpu.VMEM((4 * kpd, width), F32),
             pltpu.VMEM((ga, 4 * kpd, share), F32),
             pltpu.VMEM((nq, rows, 4 * kpd, share), F32),
-            dma((4,)), dma((ga,)),
+            dma((4, 2)), dma((ga, 2)),
             dma((3,)), dma((2, ga)),
             dma((3,)), dma((2, ga)),
             dma((2, 2)), dma((2, 2)),
-            dma((most,)), dma((rows, rows)),
+            dma((most, 2)), dma((rows, rows, 2)),
             dma, dma,
             dma((4 * rows - 1,)), dma((nq, rows)),
         ],
         compiler_params=pltpu.CompilerParams(
-            collective_id=0, has_side_effects=True, vmem_limit_bytes=64 * 1024 * 1024
+            collective_id=0, has_side_effects=True, vmem_limit_bytes=64 * 1024 * 1024 - 320 * 1024
         ),
-    )(cond_pairs, val_pairs, screened, k_plus)
+    )(cond_pairs, val_pairs, screened)
+    return pl.pallas_call(
+        functools.partial(choose, rows),
+        out_shape=(out, out),
+        in_specs=[pl.BlockSpec(memory_space=pltpu.SMEM), pl.BlockSpec(memory_space=pltpu.VMEM)],
+        out_specs=[pl.BlockSpec(memory_space=pltpu.VMEM)] * 2,
+    )(k_plus, blocks)
 
 
 NG = 1024

time: 43.5 us -> 40.8 us (0.938)
  local copies, waits for them, and re-layouts: 1.97 us -> 0 us
  Pallas kernels: 40.6 us -> 40 us
    unnamed x4 -> x0, local copies, waits for them, and re-layouts: 1.97 us -> none
    pallas_call x1 -> x2, Pallas kernels: 40.6 us -> 40 us  [the longest x1 38 us: exchanged(): pl.pallas_call(functools.partial(kernel, rows), out_shape=jax.ShapeDtypeS...]
where the time goes in v3:
time: 40.8 us; the launch traced here: 40.6 us
  Pallas kernels  40 us (98%)
  between operations  0.64 us (2%)
    pallas_call x1, Pallas kernels, exchanged(): pl.pallas_call(functools.partial(kernel, rows), out_shape=jax.ShapeDtypeS...  38 us
    pallas_call x1, Pallas kernels, exchanged(): pl.pallas_call(functools.partial(choose, rows), out_shape=(out, out), in_...  1.99 us

profile of v3, /device:TPU:0, one launch (start us, length us, event | category | flops | bytes accessed | tf_op | source)
XLA Modules:
  0.0 40.6 jit_solution(10953686373461231891)
XLA Ops:
  0.6 38.0 %shard_map.59.kall = f32[4,4,24,64]{3,2,1,0:T(8,128)} custom-call(bf16[4,6,2,16,256]{4,3,2,1,0:T(8,128)(2,1)} %c_ref.1, bf16[4,6,2,16,256]{4,3,2,1,0:T(8,128)(2,1)} %v_ref.1, bf16[4,2,128,256]{3,2,1,0:T(8,128)(2,1)} %w_ref.1), custom_call_target="tpu_custom_call" | custom-call | tf_op jit(solution)/shard_map/pallas_call | solution.py:345
  38.7 2.0 %shard_map.60 = (f32[4,6,2,64]{3,2,1,0:T(2,128)}, f32[4,6,2,64]{3,2,1,0:T(2,128)}) custom-call(s32[4,48]{1,0:T(4,128)} %kp_ref.1, f32[4,4,24,64]{3,2,1,0:T(8,128)} %shard_map.59.kall), custom_call_target="tpu_custom_call" | custom-call | tf_op jit(solution)/shard_map/pallas_call | solution.py:375

commit v4 on v3

--- a/solution.py
+++ b/solution.py
@@ -8,7 +8,6 @@
 from jax.sharding import PartitionSpec as P
 
 MESH = pl.DeviceIdType.MESH
-HIGHEST = lax.Precision.HIGHEST
 F32 = jnp.float32
 BF16 = jnp.bfloat16
 
@@ -43,6 +42,13 @@
 
 def nt(a, b):
     return lax.dot_general(a, b, (((1,), (1,)), ((), ())), preferred_element_type=F32)
+
+
+def thirds(value):
+    high = value.astype(BF16)
+    rest = value - high.astype(F32)
+    middle = rest.astype(BF16)
+    return high, middle, (rest - middle.astype(F32)).astype(BF16)
 
 
 def kernel(
@@ -237,11 +243,13 @@
     same_k = lax.div(row, npair) == lax.div(col, npair)
     vrow = lax.broadcasted_iota(jnp.int32, (mrows, width), 0)
     lane = lax.broadcasted_iota(jnp.int32, (mrows, width), 1)
-    spread = jnp.where(lax.rem(vrow, npair) == lax.rem(lane, npair), 1.0, 0.0).astype(F32)
+    spread = jnp.where(lax.rem(vrow, npair) == lax.rem(lane, npair), 1.0, 0.0).astype(BF16)
     same_a = lax.rem(vrow, npair) == lax.div(lane, npair)
     kgrid = mrows // npair
     for part, value in enumerate((kreal, kimag)):
-        wide = jnp.dot(jnp.where(same_k, value, 0.0), spread, precision=HIGHEST, preferred_element_type=F32)
+        wide = sum(
+            jnp.dot(piece, spread, preferred_element_type=F32) for piece in thirds(jnp.where(same_k, value, 0.0))
+        )
         wide = jnp.where(same_a, wide, 0.0).reshape(kgrid, npair, width)
         kown[pl.ds(part * kgrid, kgrid), :] = wide.sum(1)
 
@@ -322,10 +330,11 @@
         src_row = lax.rem(z - row_step + rows, rows)
         src_col = lax.rem(k_here - col_step + kgrid, kgrid)
         behind = jnp.where(r == src_row * 2 * kgrid + part_at + src_col, 1.0, 0.0).astype(F32)
-        for ref, choice in ((f_ref, ahead), (b_ref, behind)):
-            chosen = jnp.dot(choice, table, precision=HIGHEST, preferred_element_type=F32)
-            for t in range(kpd):
-                ref[q, t] = chosen[2 * t:2 * t + 2]
+        choice = jnp.concatenate([ahead, behind], 0).astype(BF16)
+        chosen = sum(jnp.dot(choice, piece, preferred_element_type=F32) for piece in thirds(table))
+        for t in range(kpd):
+            f_ref[q, t] = chosen[2 * t:2 * t + 2]
+            b_ref[q, t] = chosen[outs + 2 * t:outs + 2 * t + 2]
 
 
 def exchanged(cond_pairs, val_pairs, screened, k_plus):

time: 40.8 us -> 40.4 us (level)
  no operation moved by 1% of the time
where the time goes in v4:
time: 40.4 us; the launch traced here: 40.3 us
  Pallas kernels  39.6 us (98%)
  between operations  0.64 us (2%)
    pallas_call x1, Pallas kernels, exchanged(): pl.pallas_call(functools.partial(kernel, rows), out_shape=jax.ShapeDtypeS...  37.9 us
    pallas_call x1, Pallas kernels, exchanged(): pl.pallas_call(functools.partial(choose, rows), out_shape=(out, out), in_...  1.78 us

profile of v4, /device:TPU:0, one launch (start us, length us, event | category | flops | bytes accessed | tf_op | source)
XLA Modules:
  0.0 40.3 jit_solution(14349169610114500565)
XLA Ops:
  0.6 37.9 %shard_map.59.kall = f32[4,4,24,64]{3,2,1,0:T(8,128)} custom-call(bf16[4,6,2,16,256]{4,3,2,1,0:T(8,128)(2,1)} %c_ref.1, bf16[4,6,2,16,256]{4,3,2,1,0:T(8,128)(2,1)} %v_ref.1, bf16[4,2,128,256]{3,2,1,0:T(8,128)(2,1)} %w_ref.1), custom_call_target="tpu_custom_call" | custom-call | tf_op jit(solution)/shard_map/pallas_call | solution.py:354
  38.5 1.8 %shard_map.60 = (f32[4,6,2,64]{3,2,1,0:T(2,128)}, f32[4,6,2,64]{3,2,1,0:T(2,128)}) custom-call(s32[4,48]{1,0:T(4,128)} %kp_ref.1, f32[4,4,24,64]{3,2,1,0:T(8,128)} %shard_map.59.kall), custom_call_target="tpu_custom_call" | custom-call | tf_op jit(solution)/shard_map/pallas_call | solution.py:384
